TPU v7x, 32 devices: a whole 2x2x4 slice. The times are simulated.
32 devices in a mesh: modes: 8 (over z, y), gy: 4 (over x, core).
Axes of the slice: x: 2, y: 2, z: 4, core: 2. Of those that a mesh axis runs over, the one named last changes fastest.
Arguments:
- forcing: float32 [768, 16384], P('gy', 'modes'), may hold values from -6 to 6
- wavenumbers: int32 [2, 16384], P(None, 'modes'), may hold values from 0 to 7
- eigvec: float32 [4, 36864], P('gy', 'modes'), may hold values from -1 to 1, as said below
- decay: float32 [768], P('gy'), may hold values from 0.1 to 10
Outputs:
- velocity: float32 [768, 16384], P('gy', 'modes')
Inputs may be any that keep to these rules, and one draw needn't show every extreme that they name: `eigvec`: each row is an orthogonal 192 x 192 matrix stored row by row.
All inputs are finite; a program needn't handle non-finite values.
Results may differ from a plain program's by a relative error of at most 0.00027.
Values sent between devices are 32-bit elements; how exact they have to be, the bound alone decides.
A program may use at most 64 MiB of HBM per device.

v0:
```python
import functools

import jax
import jax.numpy as jnp
from jax import lax
from jax.experimental import pallas as pl
from jax.experimental.pallas import tpu as pltpu
from jax.sharding import PartitionSpec as P

coupling = 0.25
MESH = pl.DeviceIdType.MESH
LANES = 128
WIDE = 256


def split(value):
    high = value.astype(jnp.bfloat16)
    low = (value - high.astype(jnp.float32)).astype(jnp.bfloat16)
    return high, low


def product(stack, right_high, right_low):
    rows = stack.shape[0] // 2
    both = jnp.dot(stack[...], right_high, preferred_element_type=jnp.float32)
    last = jnp.dot(stack[:rows, :], right_low, preferred_element_type=jnp.float32)
    return both[:rows] + both[rows:] + last


def forward_state(q_prev, y_prev, coeffs):
    p_start, p_end, g_ss, g_se, g_ee = coeffs
    denom = 1.0 - coupling * g_ss * q_prev
    zero_part = (p_start - coupling * g_ss * y_prev) / denom
    one_part = p_end - coupling * g_se * y_prev + coupling * g_se * q_prev * zero_part
    q_zero = coupling * g_se / denom
    q_one = coupling * g_ee + coupling * g_se * q_prev * q_zero
    return (zero_part, one_part, q_zero, q_one)


def neighbour_values(parts, here, like):
    groups = len(parts)
    q_prev = y_prev = jnp.zeros_like(like)
    states = []
    for part in parts:
        state = forward_state(q_prev, y_prev, part)
        states.append(state)
        q_prev, y_prev = (state[3], state[1])
    a_next = jnp.zeros_like(like)
    mine_a = mine_b = jnp.zeros_like(like)
    for block in range(groups - 1, -1, -1):
        zero_part, one_part, q_zero, q_one = states[block]
        mine_a = jnp.where(here == block, a_next, mine_a)
        if block < groups - 1:
            mine_b = jnp.where(here == block + 1, one_part - q_one * a_next, mine_b)
        a_next = zero_part - q_zero * a_next
    return mine_a, mine_b


def send_all(count, axis, src, dst, send_sem, recv_sem):
    me = lax.axis_index(axis)
    copies = []
    for step in range(1, count):
        peer = lax.rem(me + step, count)
        copy = pltpu.make_async_remote_copy(
            src_ref=src,
            dst_ref=dst(me),
            send_sem=send_sem.at[step],
            recv_sem=recv_sem.at[step],
            device_id={axis: peer},
            device_id_type=MESH,
        )
        copy.start()
        copies.append(copy)
    return copies


def inverse(value):
    near = pl.reciprocal(value, approx=True)
    return near * (2.0 - value * near)


def kernel(
    gathers, peers, groups,
    forcing, wavenumbers, eigvec, decay,
    weight, trans, stack, rows_bc, edges,
    flat, dec, numbers, f_buf, f_high, f_low, mine, matrix,
    stack_t, g_mine, g_all, p_mine, p_all,
    in_sem, f_sem, v_send, v_recv, g_send, g_recv, p_send, p_recv,
):
    points, lines = f_buf.shape
    chunks = lines // WIDE
    me = lax.axis_index("modes")
    here = lax.axis_index("gy")
    inner = 2 if peers % 2 == 0 else 1
    outer = peers // inner
    far, near = me // inner, lax.rem(me, inner)

    barrier = pltpu.get_barrier_semaphore()
    greeted = 0
    if gathers:
        for step in range(1, outer):
            peer = lax.rem(far + step, outer) * inner + near
            pl.semaphore_signal(barrier, inc=1, device_id={"modes": peer}, device_id_type=MESH)
        for step in range(1, inner):
            peer = far * inner + lax.rem(near + step, inner)
            pl.semaphore_signal(barrier, inc=1, device_id={"modes": peer}, device_id_type=MESH)
        greeted = outer + inner - 2
    for step in range(1, groups):
        pl.semaphore_signal(
            barrier, inc=1, device_id={"gy": lax.rem(here + step, groups)}, device_id_type=MESH
        )
    eig_load = pltpu.make_async_copy(eigvec, flat.at[0] if gathers else flat, in_sem.at[0])
    eig_load.start()
    dec_load = pltpu.make_async_copy(decay, dec, in_sem.at[1])
    dec_load.start()
    num_load = pltpu.make_async_copy(wavenumbers, numbers, in_sem.at[2])
    num_load.start()
    loads = []
    for chunk in range(chunks):
        cols = pl.ds(chunk * WIDE, WIDE)
        load = pltpu.make_async_copy(forcing.at[:, cols], f_buf.at[:, cols], f_sem.at[chunk])
        load.start()
        loads.append(load)

    rows = mine.shape[1]

    def send(src, place, peer):
        copy = pltpu.make_async_remote_copy(
            src_ref=src,
            dst_ref=flat.at[place],
            send_sem=v_send.at[place],
            recv_sem=v_recv.at[place],
            device_id={"modes": peer},
            device_id_type=MESH,
        )
        copy.start()
        return copy

    def unpack(place, block):
        line = flat[place]
        for row in range(rows):
            mine[place, row:row + 1, :points] = line[:, row * points:(row + 1) * points]
        matrix[pl.ds(pl.multiple_of(block * rows, 8), rows), :] = mine[place]

    def near_peer(turn):
        return far * inner + lax.rem(near + turn, inner)

    hops = {}
    if gathers:
        pl.semaphore_wait(barrier, greeted + groups - 1)
        for step in range(1, outer):
            hops[step] = send(eigvec, step, lax.rem(far + step, outer) * inner + near)
        for turn in range(1, inner):
            hops[turn * outer] = send(eigvec, turn * outer, near_peer(turn))
        eig_load.wait()
        unpack(0, me)
    else:
        pl.semaphore_wait(barrier, groups - 1)
        eig_load.wait()
        matrix[:, :points] = flat[...]

    dec_load.wait()
    num_load.wait()
    row_at = lax.broadcasted_iota(jnp.int32, (points, points), 0)
    col_at = lax.broadcasted_iota(jnp.int32, (points, points), 1)
    rate = jnp.sum(jnp.where(row_at == col_at, dec[...], 0.0), axis=1, keepdims=True)
    rate = jnp.broadcast_to(rate, (points, LANES))
    for chunk in range(lines // LANES):
        cols = slice(chunk * LANES, (chunk + 1) * LANES)
        kx = numbers[0:1, cols].astype(jnp.float32) / 64.0
        kz = numbers[1:2, cols].astype(jnp.float32) / 24.0
        weight[:, cols] = inverse(kx * kx + kz * kz + rate)
    if gathers:
        for step in range(1, outer):
            hops[step].wait_recv()
            for turn in range(1, inner):
                place = turn * outer + step
                hops[place] = send(flat.at[step], place, near_peer(turn))
        for step in range(1, outer):
            unpack(step, lax.rem(far + outer - step, outer) * inner + near)
    for chunk in range(chunks):
        cols = slice(chunk * WIDE, (chunk + 1) * WIDE)
        loads[chunk].wait()
        f_high[:, cols], f_low[:, cols] = split(f_buf[:, cols])
    if gathers:
        for turn in range(1, inner):
            for step in range(outer):
                place = turn * outer + step
                hops[place].wait_recv()
                unpack(
                    place,
                    lax.rem(far + outer - step, outer) * inner + lax.rem(near + inner - turn, inner),
                )
        for copy in hops.values():
            copy.wait_send()
    full = matrix[:, :points]
    stack[:points, :], stack[points:, :] = split(full)
    turned = full.T
    stack_t[:points, :], stack_t[points:, :] = split(turned)
    first = jnp.broadcast_to(turned[:, 0:1], (points, LANES))
    last = jnp.broadcast_to(turned[:, points - 1:points], (points, LANES))
    rows_bc[0] = first
    rows_bc[1] = last
    rows_bc[2] = first * first
    rows_bc[3] = first * last
    rows_bc[4] = last * last

    per = WIDE // LANES
    g_copies = []
    for chunk in range(chunks):
        cols = slice(chunk * WIDE, (chunk + 1) * WIDE)
        if 2 * chunk < chunks:
            for row in range(2 * chunk * per, min(2 * chunk + 2, chunks) * per):
                part = weight[:, row * LANES:(row + 1) * LANES]
                for which in range(3):
                    g_mine[which, row:row + 1, :] = jnp.sum(
                        rows_bc[2 + which] * part, axis=0, keepdims=True
                    )
            if 2 * chunk + 2 >= chunks:
                g_copies = send_all(groups, "gy", g_mine, lambda at: g_all.at[at], g_send, g_recv)
                g_all[here] = g_mine[...]
        value = product(stack_t, f_high[:, cols], f_low[:, cols])
        trans[:, cols] = value
        scaled = value * weight[:, cols]
        for half in range(WIDE // LANES):
            part = scaled[:, half * LANES:(half + 1) * LANES]
            row = chunk * (WIDE // LANES) + half
            for which in range(2):
                p_mine[which, row:row + 1, :] = jnp.sum(rows_bc[which] * part, axis=0, keepdims=True)
    p_copies = send_all(groups, "gy", p_mine, lambda at: p_all.at[at], p_send, p_recv)
    p_all[here] = p_mine[...]

    for copy in g_copies:
        copy.wait()
    for copy in p_copies:
        copy.wait()
    parts = [
        (p_all[block, 0], p_all[block, 1], g_all[block, 0], g_all[block, 1], g_all[block, 2])
        for block in range(groups)
    ]
    a_next, b_prev = neighbour_values(parts, here, parts[0][0])
    edges[0] = coupling * a_next
    edges[1] = coupling * b_prev


def finish(weight, trans, stack, rows_bc, edges, out, result, sem):
    points, lines = trans.shape
    stores = []
    for chunk in range(lines // WIDE):
        halves = []
        for half in range(WIDE // LANES):
            row = chunk * (WIDE // LANES) + half
            lane = slice(row * LANES, (row + 1) * LANES)
            bare = (
                trans[:, lane]
                - edges[0, row:row + 1, :] * rows_bc[1]
                - edges[1, row:row + 1, :] * rows_bc[0]
            )
            halves.append(weight[:, lane] * bare)
        high, low = split(jnp.concatenate(halves, axis=1))
        span = pl.ds(chunk * WIDE, WIDE)
        result[:, span] = product(stack, high, low)
        store = pltpu.make_async_copy(result.at[:, span], out.at[:, span], sem.at[chunk])
        store.start()
        stores.append(store)
    for store in stores:
        store.wait()


def local(peers, groups, forcing, wavenumbers, eigvec, decay):
    points, lines = forcing.shape
    held = eigvec.shape[1]
    gathers = held % (8 * points) == 0
    if not gathers:
        eigvec = lax.all_gather(eigvec, "modes", axis=1, tiled=True).reshape(points, points)
    rows = held // points if gathers else 8
    f32, bf16 = jnp.float32, jnp.bfloat16
    tall = lines // LANES
    padded = -(-points // LANES) * LANES
    chunks = lines // WIDE
    dma = pltpu.SemaphoreType.DMA
    vmem = pl.BlockSpec(memory_space=pltpu.VMEM)
    hbm = pl.BlockSpec(memory_space=pltpu.HBM)
    solved = pl.pallas_call(
        functools.partial(kernel, gathers, peers, groups),
        out_shape=(
            jax.ShapeDtypeStruct((points, lines), f32),
            jax.ShapeDtypeStruct((points, lines), f32),
            jax.ShapeDtypeStruct((2 * points, points), bf16),
            jax.ShapeDtypeStruct((5, points, LANES), f32),
            jax.ShapeDtypeStruct((2, tall, LANES), f32),
        ),
        in_specs=[hbm, hbm, hbm, hbm],
        out_specs=(vmem,) * 5,
        scratch_shapes=[
            pltpu.VMEM((peers, *eigvec.shape) if gathers else eigvec.shape, f32),
            pltpu.VMEM((1, points), f32),
            pltpu.VMEM(wavenumbers.shape, jnp.int32),
            pltpu.VMEM((points, lines), f32),
            pltpu.VMEM((points, lines), bf16),
            pltpu.VMEM((points, lines), bf16),
            pltpu.VMEM((peers if gathers else 1, rows, padded), f32),
            pltpu.VMEM((points, padded), f32),
            pltpu.VMEM((2 * points, points), bf16),
            pltpu.VMEM((3, tall, LANES), f32),
            pltpu.VMEM((groups, 3, tall, LANES), f32),
            pltpu.VMEM((2, tall, LANES), f32),
            pltpu.VMEM((groups, 2, tall, LANES), f32),
            dma((3,)),
            dma((chunks,)),
            dma((peers,)),
            dma((peers,)),
            dma((groups,)),
            dma((groups,)),
            dma((groups,)),
            dma((groups,)),
        ],
        compiler_params=pltpu.CompilerParams(
            collective_id=0, has_side_effects=True, vmem_limit_bytes=32 * 1024 * 1024
        ),
        name="helmholtz",
    )(*[
        pltpu.with_memory_space_constraint(operand, pltpu.HBM)
        for operand in (forcing, wavenumbers, eigvec, decay.reshape(1, points))
    ])
    return pl.pallas_call(
        finish,
        out_shape=jax.ShapeDtypeStruct((points, lines), f32),
        in_specs=[vmem] * 5,
        out_specs=hbm,
        scratch_shapes=[pltpu.VMEM((points, lines), f32), dma((chunks,))],
        compiler_params=pltpu.CompilerParams(vmem_limit_bytes=16 * 1024 * 1024),
        name="finish",
    )(*solved)


def solution(mesh):
    placed = (P("gy", "modes"), P(None, "modes"), P("gy", "modes"), P("gy"))
    return jax.shard_map(
        functools.partial(local, mesh.shape["modes"], mesh.shape["gy"]),
        mesh=mesh, in_specs=placed, out_specs=P("gy", "modes"), check_vma=False,
    )
```

profile of v0, /device:TPU:0, one launch (start us, length us, event | category | flops | bytes accessed | tf_op | source)
XLA Modules:
  0.0 18.3 jit_solution(7744447843977309496)
XLA Ops:
  0.0 16.6 %helmholtz.1 = (f32[192,2048]{1,0:T(8,128)S(1)}, f32[192,2048]{1,0:T(8,128)S(1)}, bf16[384,192]{1,0:T(8,128)(2,1)S(1)}, f32[5,192,128]{2,1,0:T(8,128)S(1)}, f32[2,16,128]{2,1,0:T(8,128)S(1)}) custom-call(f32[192,2048]{1,0:T(8,128)} %forcing.1, s32[2,2048]{1,0:T(2,128)} %wavenumbers.1, f32[1,4608]{1,0:T(1,128)} %eigvec.1, f32[1,192]{1,0:T(1,128)} %bitcast.1), custom_call_target="tpu_custom_call" | custom-call | tf_op jit(solution)/shard_map/helmholtz/pallas_call | solution.py:283
  16.6 1.7 %finish.1 = f32[192,2048]{1,0:T(8,128)} custom-call(f32[192,2048]{1,0:T(8,128)S(1)} %get-tuple-element.10.weight, f32[192,2048]{1,0:T(8,128)S(1)} %get-tuple-element.11.trans, bf16[384,192]{1,0:T(8,128)(2,1)S(1)} %get-tuple-element.12.stack, f32[5,192,128]{2,1,0:T(8,128)S(1)} %get-tuple-element.13.rows_bc, f32[2,16,128]{2,1,0:T(8,128)S(1)} %get-tuple-element.14.edges), custom_call_target="tpu_custom_call" | custom-call | tf_op jit(solution)/shard_map/finish/pallas_call | solution.py:325
where the time goes:
time: 18.4 us; the launch traced here: 18.3 us
  Pallas kernels  18.3 us (99%)
    pallas_call x1, Pallas kernels, local(): pl.pallas_call(functools.partial(kernel, gathers, peers, groups), out_sha...  16.6 us
    pallas_call x1, Pallas kernels, local(): pl.pallas_call(finish, out_shape=jax.ShapeDtypeStruct((points, lines), f3...  1.72 us

commit v1 on v0

--- a/solution.py
+++ b/solution.py
@@ -26,28 +26,32 @@
     return both[:rows] + both[rows:] + last
 
 
-def forward_state(q_prev, y_prev, coeffs):
-    p_start, p_end, g_ss, g_se, g_ee = coeffs
-    denom = 1.0 - coupling * g_ss * q_prev
-    zero_part = (p_start - coupling * g_ss * y_prev) / denom
-    one_part = p_end - coupling * g_se * y_prev + coupling * g_se * q_prev * zero_part
-    q_zero = coupling * g_se / denom
-    q_one = coupling * g_ee + coupling * g_se * q_prev * q_zero
-    return (zero_part, one_part, q_zero, q_one)
-
-
-def neighbour_values(parts, here, like):
-    groups = len(parts)
-    q_prev = y_prev = jnp.zeros_like(like)
+def corner_states(corners):
+    q_prev = jnp.zeros_like(corners[0][0])
     states = []
-    for part in parts:
-        state = forward_state(q_prev, y_prev, part)
-        states.append(state)
-        q_prev, y_prev = (state[3], state[1])
-    a_next = jnp.zeros_like(like)
-    mine_a = mine_b = jnp.zeros_like(like)
+    for g_ss, g_se, g_ee in corners:
+        scale = 1.0 / (1.0 - coupling * g_ss * q_prev)
+        q_zero = coupling * g_se * scale
+        q_one = coupling * g_ee + coupling * g_se * q_prev * q_zero
+        states.append((scale, coupling * g_ss, coupling * g_se, coupling * g_se * q_prev, q_zero, q_one))
+        q_prev = q_one
+    return states
+
+
+def neighbour_values(states, edge_values, here):
+    groups = len(states)
+    zero = jnp.zeros_like(edge_values[0][0])
+    y_prev = zero
+    values = []
+    for (p_start, p_end), (scale, c_ss, c_se, c_seq, _, _) in zip(edge_values, states):
+        zero_part = (p_start - c_ss * y_prev) * scale
+        one_part = p_end - c_se * y_prev + c_seq * zero_part
+        values.append((zero_part, one_part))
+        y_prev = one_part
+    a_next = mine_a = mine_b = zero
     for block in range(groups - 1, -1, -1):
-        zero_part, one_part, q_zero, q_one = states[block]
+        zero_part, one_part = values[block]
+        q_zero, q_one = states[block][4:]
         mine_a = jnp.where(here == block, a_next, mine_a)
         if block < groups - 1:
             mine_b = jnp.where(here == block + 1, one_part - q_one * a_next, mine_b)
@@ -90,20 +94,15 @@
     chunks = lines // WIDE
     me = lax.axis_index("modes")
     here = lax.axis_index("gy")
-    inner = 2 if peers % 2 == 0 else 1
-    outer = peers // inner
-    far, near = me // inner, lax.rem(me, inner)
 
     barrier = pltpu.get_barrier_semaphore()
     greeted = 0
     if gathers:
-        for step in range(1, outer):
-            peer = lax.rem(far + step, outer) * inner + near
-            pl.semaphore_signal(barrier, inc=1, device_id={"modes": peer}, device_id_type=MESH)
-        for step in range(1, inner):
-            peer = far * inner + lax.rem(near + step, inner)
-            pl.semaphore_signal(barrier, inc=1, device_id={"modes": peer}, device_id_type=MESH)
-        greeted = outer + inner - 2
+        for step in range(1, peers):
+            pl.semaphore_signal(
+                barrier, inc=1, device_id={"modes": lax.rem(me + step, peers)}, device_id_type=MESH
+            )
+        greeted = peers - 1
     for step in range(1, groups):
         pl.semaphore_signal(
             barrier, inc=1, device_id={"gy": lax.rem(here + step, groups)}, device_id_type=MESH
@@ -123,35 +122,27 @@
 
     rows = mine.shape[1]
 
-    def send(src, place, peer):
-        copy = pltpu.make_async_remote_copy(
-            src_ref=src,
-            dst_ref=flat.at[place],
-            send_sem=v_send.at[place],
-            recv_sem=v_recv.at[place],
-            device_id={"modes": peer},
-            device_id_type=MESH,
-        )
-        copy.start()
-        return copy
-
     def unpack(place, block):
         line = flat[place]
         for row in range(rows):
             mine[place, row:row + 1, :points] = line[:, row * points:(row + 1) * points]
         matrix[pl.ds(pl.multiple_of(block * rows, 8), rows), :] = mine[place]
 
-    def near_peer(turn):
-        return far * inner + lax.rem(near + turn, inner)
-
-    hops = {}
+    hops = []
     if gathers:
+        eig_load.wait()
         pl.semaphore_wait(barrier, greeted + groups - 1)
-        for step in range(1, outer):
-            hops[step] = send(eigvec, step, lax.rem(far + step, outer) * inner + near)
-        for turn in range(1, inner):
-            hops[turn * outer] = send(eigvec, turn * outer, near_peer(turn))
-        eig_load.wait()
+        for step in range(1, peers):
+            copy = pltpu.make_async_remote_copy(
+                src_ref=flat.at[0],
+                dst_ref=flat.at[step],
+                send_sem=v_send.at[step],
+                recv_sem=v_recv.at[step],
+                device_id={"modes": lax.rem(me + step, peers)},
+                device_id_type=MESH,
+            )
+            copy.start()
+            hops.append(copy)
         unpack(0, me)
     else:
         pl.semaphore_wait(barrier, groups - 1)
@@ -169,29 +160,15 @@
         kx = numbers[0:1, cols].astype(jnp.float32) / 64.0
         kz = numbers[1:2, cols].astype(jnp.float32) / 24.0
         weight[:, cols] = inverse(kx * kx + kz * kz + rate)
-    if gathers:
-        for step in range(1, outer):
-            hops[step].wait_recv()
-            for turn in range(1, inner):
-                place = turn * outer + step
-                hops[place] = send(flat.at[step], place, near_peer(turn))
-        for step in range(1, outer):
-            unpack(step, lax.rem(far + outer - step, outer) * inner + near)
     for chunk in range(chunks):
         cols = slice(chunk * WIDE, (chunk + 1) * WIDE)
         loads[chunk].wait()
         f_high[:, cols], f_low[:, cols] = split(f_buf[:, cols])
-    if gathers:
-        for turn in range(1, inner):
-            for step in range(outer):
-                place = turn * outer + step
-                hops[place].wait_recv()
-                unpack(
-                    place,
-                    lax.rem(far + outer - step, outer) * inner + lax.rem(near + inner - turn, inner),
-                )
-        for copy in hops.values():
-            copy.wait_send()
+    for step, copy in enumerate(hops, 1):
+        copy.wait_recv()
+        unpack(step, lax.rem(me + peers - step, peers))
+    for copy in hops:
+        copy.wait_send()
     full = matrix[:, :points]
     stack[:points, :], stack[points:, :] = split(full)
     turned = full.T
@@ -231,13 +208,14 @@
 
     for copy in g_copies:
         copy.wait()
+    states = corner_states(
+        [(g_all[block, 0], g_all[block, 1], g_all[block, 2]) for block in range(groups)]
+    )
     for copy in p_copies:
         copy.wait()
-    parts = [
-        (p_all[block, 0], p_all[block, 1], g_all[block, 0], g_all[block, 1], g_all[block, 2])
-        for block in range(groups)
-    ]
-    a_next, b_prev = neighbour_values(parts, here, parts[0][0])
+    a_next, b_prev = neighbour_values(
+        states, [(p_all[block, 0], p_all[block, 1]) for block in range(groups)], here
+    )
     edges[0] = coupling * a_next
     edges[1] = coupling * b_prev
 

time: 18.4 us -> 16.6 us (0.902)
  Pallas kernels: 18.3 us -> 16.4 us
    pallas_call x1, Pallas kernels: 16.6 us -> 14.7 us  [local(): pl.pallas_call(functools.partial(kernel, gathers, peers, groups), out_sha...]
where the time goes in v1:
time: 16.6 us; the launch traced here: 16.4 us
  Pallas kernels  16.4 us (99%)
    pallas_call x1, Pallas kernels, local(): pl.pallas_call(functools.partial(kernel, gathers, peers, groups), out_sha...  14.7 us
    pallas_call x1, Pallas kernels, local(): pl.pallas_call(finish, out_shape=jax.ShapeDtypeStruct((points, lines), f3...  1.71 us

profile of v1, /device:TPU:0, one launch (start us, length us, event | category | flops | bytes accessed | tf_op | source)
XLA Modules:
  0.0 16.4 jit_solution(6169787041841315248)
XLA Ops:
  0.0 14.7 %helmholtz.1 = (f32[192,2048]{1,0:T(8,128)S(1)}, f32[192,2048]{1,0:T(8,128)S(1)}, bf16[384,192]{1,0:T(8,128)(2,1)S(1)}, f32[5,192,128]{2,1,0:T(8,128)S(1)}, f32[2,16,128]{2,1,0:T(8,128)S(1)}) custom-call(f32[192,2048]{1,0:T(8,128)} %forcing.1, s32[2,2048]{1,0:T(2,128)} %wavenumbers.1, f32[1,4608]{1,0:T(1,128)} %eigvec.1, f32[1,192]{1,0:T(1,128)} %bitcast.1), custom_call_target="tpu_custom_call" | custom-call | tf_op jit(solution)/shard_map/helmholtz/pallas_call | solution.py:261
  14.7 1.7 %finish.1 = f32[192,2048]{1,0:T(8,128)} custom-call(f32[192,2048]{1,0:T(8,128)S(1)} %get-tuple-element.10.weight, f32[192,2048]{1,0:T(8,128)S(1)} %get-tuple-element.11.trans, bf16[384,192]{1,0:T(8,128)(2,1)S(1)} %get-tuple-element.12.stack, f32[5,192,128]{2,1,0:T(8,128)S(1)} %get-tuple-element.13.rows_bc, f32[2,16,128]{2,1,0:T(8,128)S(1)} %get-tuple-element.14.edges), custom_call_target="tpu_custom_call" | custom-call | tf_op jit(solution)/shard_map/finish/pallas_call | solution.py:303

commit v2 on v1

--- a/solution.py
+++ b/solution.py
@@ -132,7 +132,7 @@
     if gathers:
         eig_load.wait()
         pl.semaphore_wait(barrier, greeted + groups - 1)
-        for step in range(1, peers):
+        for step in sorted(range(1, peers), key=lambda at: abs(2 * at - peers)):
             copy = pltpu.make_async_remote_copy(
                 src_ref=flat.at[0],
                 dst_ref=flat.at[step],
@@ -142,7 +142,7 @@
                 device_id_type=MESH,
             )
             copy.start()
-            hops.append(copy)
+            hops.append((step, copy))
         unpack(0, me)
     else:
         pl.semaphore_wait(barrier, groups - 1)
@@ -164,11 +164,9 @@
         cols = slice(chunk * WIDE, (chunk + 1) * WIDE)
         loads[chunk].wait()
         f_high[:, cols], f_low[:, cols] = split(f_buf[:, cols])
-    for step, copy in enumerate(hops, 1):
+    for step, copy in hops:
         copy.wait_recv()
         unpack(step, lax.rem(me + peers - step, peers))
-    for copy in hops:
-        copy.wait_send()
     full = matrix[:, :points]
     stack[:points, :], stack[points:, :] = split(full)
     turned = full.T
@@ -207,17 +205,19 @@
     p_all[here] = p_mine[...]
 
     for copy in g_copies:
-        copy.wait()
+        copy.wait_recv()
     states = corner_states(
         [(g_all[block, 0], g_all[block, 1], g_all[block, 2]) for block in range(groups)]
     )
     for copy in p_copies:
-        copy.wait()
+        copy.wait_recv()
     a_next, b_prev = neighbour_values(
         states, [(p_all[block, 0], p_all[block, 1]) for block in range(groups)], here
     )
     edges[0] = coupling * a_next
     edges[1] = coupling * b_prev
+    for copy in [copy for _, copy in hops] + g_copies + p_copies:
+        copy.wait_send()
 
 
 def finish(weight, trans, stack, rows_bc, edges, out, result, sem):

time: 16.6 us -> 17.3 us (1.042)
  Pallas kernels: 16.4 us -> 17.2 us
    pallas_call x1, Pallas kernels: 14.7 us -> 15.5 us  [local(): pl.pallas_call(functools.partial(kernel, gathers, peers, groups), out_sha...]
where the time goes in v2:
time: 17.3 us; the launch traced here: 17.2 us
  Pallas kernels  17.2 us (99%)
    pallas_call x1, Pallas kernels, local(): pl.pallas_call(functools.partial(kernel, gathers, peers, groups), out_sha...  15.5 us
    pallas_call x1, Pallas kernels, local(): pl.pallas_call(finish, out_shape=jax.ShapeDtypeStruct((points, lines), f3...  1.72 us

profile of v2, /device:TPU:0, one launch (start us, length us, event | category | flops | bytes accessed | tf_op | source)
XLA Modules:
  0.0 17.2 jit_solution(13078572696970622869)
XLA Ops:
  0.0 15.5 %helmholtz.1 = (f32[192,2048]{1,0:T(8,128)S(1)}, f32[192,2048]{1,0:T(8,128)S(1)}, bf16[384,192]{1,0:T(8,128)(2,1)S(1)}, f32[5,192,128]{2,1,0:T(8,128)S(1)}, f32[2,16,128]{2,1,0:T(8,128)S(1)}) custom-call(f32[192,2048]{1,0:T(8,128)} %forcing.1, s32[2,2048]{1,0:T(2,128)} %wavenumbers.1, f32[1,4608]{1,0:T(1,128)} %eigvec.1, f32[1,192]{1,0:T(1,128)} %bitcast.1), custom_call_target="tpu_custom_call" | custom-call | tf_op jit(solution)/shard_map/helmholtz/pallas_call | solution.py:261
  15.5 1.7 %finish.1 = f32[192,2048]{1,0:T(8,128)} custom-call(f32[192,2048]{1,0:T(8,128)S(1)} %get-tuple-element.10.weight, f32[192,2048]{1,0:T(8,128)S(1)} %get-tuple-element.11.trans, bf16[384,192]{1,0:T(8,128)(2,1)S(1)} %get-tuple-element.12.stack, f32[5,192,128]{2,1,0:T(8,128)S(1)} %get-tuple-element.13.rows_bc, f32[2,16,128]{2,1,0:T(8,128)S(1)} %get-tuple-element.14.edges), custom_call_target="tpu_custom_call" | custom-call | tf_op jit(solution)/shard_map/finish/pallas_call | solution.py:303
